TPU v7x, 32 devices: a whole 2x2x4 slice. The times are simulated.
32 devices in a mesh: row: 16 (over z, x, core), col: 2 (over y).
Axes of the slice: x: 2, y: 2, z: 4, core: 2. Of those that a mesh axis runs over, the one named last changes fastest.
Arguments:
- gbar: float32 [8192, 8192], P('row', 'col'), may hold values from -9 to 9
- panels: float32 [8192, 1024], P('row'), may hold values from -0.0625 to 0.0625
- panel_cot: float32 [8192, 1024], P('row'), may hold values from -6 to 6
- inverses: float32 [2, 512, 512], replicated, may hold values from -1 to 2, as said below
Outputs:
- adjoint: float32 [8192, 1024], P('row')
- diag_adjoint: float32 [2, 512, 512], P(None, 'row')
Inputs may be any that keep to these rules, and one draw needn't show every extreme that they name: Each inverses[i] is lower triangular with diagonal entries between 1 and 2.
All inputs are finite; a program needn't handle non-finite values.
Results may differ from a plain program's by a relative error of at most 0.000071.
Values sent between devices are 32-bit elements; how exact they have to be, the bound alone decides.
A program may use at most 128 MiB of HBM per device.

v0:
```python
import jax
import jax.numpy as jnp
from jax import lax
from jax.sharding import PartitionSpec as P


def spread(value, axis, source):
    kept = jnp.where(lax.axis_index(axis) == source, value, 0).astype(value.dtype)
    return lax.psum(kept, axis)


def per_device(gbar, panels, panel_cot, inverses):
    width = inverses.shape[-1]
    exact_mode = lax.Precision.HIGHEST
    row_id = lax.axis_index("row")
    col_count = lax.axis_size("col")
    partial_value = lax.dot_general(
        gbar,
        panels,
        (((0,), (0,)), ((), ())),
        precision=exact_mode,
        preferred_element_type=jnp.float32,
    )
    summed = lax.psum(partial_value, "row")
    own_tile = lax.dynamic_slice_in_dim(summed, row_id // col_count * width, width, 0)
    coupled = spread(own_tile, "col", row_id % col_count)
    combined = panel_cot - 2.0 * coupled
    first_adj = jnp.dot(
        combined[:, :width], inverses[0], precision=exact_mode, preferred_element_type=jnp.float32
    )
    second_adj = jnp.dot(
        combined[:, width:], inverses[1], precision=exact_mode, preferred_element_type=jnp.float32
    )
    adjoint = jnp.concatenate([first_adj, second_adj], axis=1)
    contract = (((0,), (0,)), ((), ()))
    first_diag = -lax.dot_general(
        first_adj,
        panels[:, :width],
        contract,
        precision=exact_mode,
        preferred_element_type=jnp.float32,
    )
    second_diag = -lax.dot_general(
        second_adj,
        panels[:, width:],
        contract,
        precision=exact_mode,
        preferred_element_type=jnp.float32,
    )
    diag_terms = jnp.stack([first_diag, second_diag])
    diag_adjoint = lax.psum_scatter(diag_terms, "row", scatter_dimension=1, tiled=True)
    return (adjoint, diag_adjoint)


def solution(mesh):
    in_specs = (P("row", "col"), P("row", None), P("row", None), P())
    out_specs = (P("row", None), P(None, "row", None))
    return jax.shard_map(
        per_device, mesh=mesh, in_specs=in_specs, out_specs=out_specs, check_vma=False
    )
```

profile of v0, /device:TPU:0, one launch (start us, length us, event | category | flops | bytes accessed | tf_op | source)
XLA Modules:
  0.0 485.4 jit_solution(16080054003184823967)
XLA Ops:
  7.2 0.0 all-reduce.3.cloned.1.call-start
  7.2 31.4 %fusion.12 = f32[4096,1024]{1,0:T(8,128)} fusion(f32[512,4096]{1,0:T(8,128)} %param.4, f32[512,1024]{1,0:T(8,128)} %param.5), kind=kOutput, calls=%fused_computation.18 | convolution fusion | flops 25769803776 | bytes 27262976 | tf_op jit(solution)/shard_map/dot_general | solution.py:17
  38.6 0.0 all-reduce.3.cloned.1.call-update
  38.6 0.0 all-reduce.5.cloned.1.call-start
  38.7 301.0 %all-reduce.3.cloned.1.call-done = f32[4096,1024]{1,0:T(8,128)} async-done(((f32[4096,1024]{1,0:T(8,128)}), f32[4096,1024]{1,0:T(8,128)}) %all-reduce.3.cloned.1.call-update) | async-done | bytes 16777232 | tf_op jit(solution)/shard_map/psum | solution.py:24
  339.8 3.2 dynamic-slice_select_fusion
  343.0 0.0 copy-start.1
  343.0 0.0 all-reduce.5.cloned.1.call-update
  343.0 0.2 reduce-scatter.2.cloned.1.call-start
  343.2 62.6 %all-reduce.5.cloned.1.call-done = f32[512,1024]{1,0:T(8,128)} async-done(((f32[512,1024]{1,0:T(8,128)}), f32[512,1024]{1,0:T(8,128)}) %all-reduce.5.cloned.1.call-update) | async-done | bytes 2097168 | tf_op jit(solution)/shard_map/psum | solution.py:9
  405.8 0.0 copy-done.1
  405.8 0.0 copy-start.2
  405.8 2.2 multiply_subtract_fusion
  408.0 0.1 copy-done.2
  408.0 1.9 fusion.2
  409.9 0.0 copy-start
  410.0 1.9 fusion.4
  411.9 0.0 copy-done
  411.9 1.9 fusion
  413.7 1.9 fusion.1
  415.6 1.5 pad_maximum_fusion.1
  417.1 0.0 reduce-scatter.2.cloned.1.call-update
  417.1 1.5 pad_maximum_fusion
  418.6 2.9 copy.6
  421.5 57.3 %reduce-scatter.2.cloned.1.call-done = f32[2,32,512]{2,1,0:T(8,128)} async-done(((f32[2,512,512]{2,1,0:T(8,128)}), f32[2,32,512]{2,1,0:T(8,128)}) %reduce-scatter.2.cloned.1.call-update) | async-done | bytes 131088 | tf_op jit(solution)/shard_map/reduce_scatter | solution.py:51
Async XLA Ops:
  7.2 332.6 %all-reduce.3.cloned.1.call-start = ((), (), s32[]{:S(2)}) async-start(), calls=%async_computation.1 | async-start | bytes 33554432 | tf_op jit(solution)/shard_map/psum | solution.py:24
  38.6 367.2 %all-reduce.5.cloned.1.call-start = ((), (), s32[]{:S(2)}) async-start(), calls=%async_computation.2 | async-start | bytes 4194304 | tf_op jit(solution)/shard_map/psum | solution.py:9
  343.0 62.9 %copy-start.1 = (f32[512,1024]{1,0:T(8,128)S(1)}, f32[512,1024]{1,0:T(8,128)}, u32[]{:S(2)}) copy-start(f32[512,1024]{1,0:T(8,128)} %param.6) | copy-start | bytes 6291460
  343.0 135.9 %reduce-scatter.2.cloned.1.call-start = ((), (), s32[]{:S(2)}) async-start(), calls=%async_computation.3 | async-start | bytes 2228224 | tf_op jit(solution)/shard_map/reduce_scatter | solution.py:51
  405.8 2.2 copy-start.2
  409.9 1.9 copy-start
Sparse Core Ops, SparseCore 0:
  38.8 300.9 all-reduce.2
  343.1 62.6 all-reduce.4
  417.3 61.5 reduce-scatter.1
where the time goes:
time: 486 us; the launch traced here: 485 us
  waiting for transfers between devices  421 us (87%)
  matrix products  38.9 us (8%)
  between operations  13.8 us (3%)
  other arithmetic  8.34 us (2%)
    psum x1, waiting for transfers between devices, per_device(): summed = lax.psum(partial_value, 'row')  301 us
    psum x1, waiting for transfers between devices, spread(): return lax.psum(kept, axis)  62.6 us
    reduce_scatter x1, waiting for transfers between devices, per_device(): lax.psum_scatter(diag_terms, 'row', scatter_dimension=1, tiled=True)  57.3 us
    dot_general x1, matrix products, per_device(): lax.dot_general(gbar, panels, (((0,), (0,)), ((), ())), precision=exact_m...  31.4 us
  transfers between devices with their start and end apart: 3, of which 3 were waited for; matrix products, arithmetic and copies ran while one was open for 1% of the time, Pallas kernels for 0%

commit v1 on v0

--- a/solution.py
+++ b/solution.py
@@ -21,7 +21,9 @@
         precision=exact_mode,
         preferred_element_type=jnp.float32,
     )
-    summed = lax.psum(partial_value, "row")
+    summed = partial_value
+    for hop in (1, 2, 4, 8):
+        summed = summed + lax.ppermute(summed, "row", [(dev, dev ^ hop) for dev in range(16)])
     own_tile = lax.dynamic_slice_in_dim(summed, row_id // col_count * width, width, 0)
     coupled = spread(own_tile, "col", row_id % col_count)
     combined = panel_cot - 2.0 * coupled

time: 486 us -> 1700 us (3.50)
  waiting for transfers between devices: 421 us -> 1590 us
  other arithmetic: 8.34 us -> 46 us
    ppermute x0 -> x4, waiting for transfers between devices: none -> 1460 us  [per_device(): lax.ppermute(summed, 'row', [(dev, dev ^ hop) for dev in range(16)])]
    psum x1 -> x0, waiting for transfers between devices: 301 us -> none  [per_device(): summed = lax.psum(partial_value, 'row')]
    add x0 -> x3, other arithmetic: none -> 36.6 us  [per_device(): summed + lax.ppermute(summed, 'row', [(dev, dev ^ hop) for dev in range(1...]
  transfers between devices with their start and end apart: 3 -> 6, of which waited for: 3 -> 6; matrix products, arithmetic and copies ran while one was open for 1% -> 0% of each run, Pallas kernels for 0% -> 0%
where the time goes in v1:
time: 1700 us
  waiting for transfers between devices  1590 us (94%)
  other arithmetic  46 us (3%)
  matrix products  38.7 us (2%)
    ppermute x4, waiting for transfers between devices, per_device(): lax.ppermute(summed, 'row', [(dev, dev ^ hop) for dev in range(16)])  1460 us
    psum x1, waiting for transfers between devices, spread(): return lax.psum(kept, axis)  63.6 us
    reduce_scatter x1, waiting for transfers between devices, per_device(): lax.psum_scatter(diag_terms, 'row', scatter_dimension=1, tiled=True)  57.3 us
    add x3, other arithmetic, per_device(): summed + lax.ppermute(summed, 'row', [(dev, dev ^ hop) for dev in range(1...  36.6 us
  transfers between devices with their start and end apart: 6, of which 6 were waited for; matrix products, arithmetic and copies ran while one was open for 0% of the time, Pallas kernels for 0%

profile of v1, /device:TPU:0, one launch (start us, length us, event | category | flops | bytes accessed | tf_op | source)
XLA Modules:
  0.0 1695.5 jit_solution(12458530291625175999)
XLA Ops:
  7.2 0.0 all-reduce.2.cloned.1.call-start
  7.2 31.1 %fusion.13 = f32[4096,1024]{1,0:T(8,128)S(1)} fusion(f32[512,4096]{1,0:T(8,128)} %param.4, f32[512,1024]{1,0:T(8,128)} %param.5), kind=kOutput, calls=%fused_computation.19 | convolution fusion | flops 25769803776 | bytes 27262976 | tf_op jit(solution)/shard_map/dot_general | solution.py:17
  38.4 0.5 collective-permute-start
  38.9 24.9 %collective-permute-done = f32[4096,1024]{1,0:T(8,128)} collective-permute-done((f32[4096,1024]{1,0:T(8,128)S(1)}, f32[4096,1024]{1,0:T(8,128)}, u32[]{:S(2)}, u32[]{:S(2)}) %collective-permute-start) | collective-permute-done | bytes 16777248 | tf_op jit(solution)/shard_map/ppermute | solution.py:26
  63.8 12.4 add.25
  76.2 2.9 collective-permute-start.1
  79.1 360.8 %collective-permute-done.1 = f32[4096,1024]{1,0:T(8,128)} collective-permute-done((f32[4096,1024]{1,0:T(8,128)}, f32[4096,1024]{1,0:T(8,128)}, u32[]{:S(2)}, u32[]{:S(2)}) %collective-permute-start.1) | collective-permute-done | bytes 16777248 | tf_op jit(solution)/shard_map/ppermute | solution.py:26
  439.9 11.8 add.26
  451.7 1.9 collective-permute-start.2
  453.6 360.0 %collective-permute-done.2 = f32[4096,1024]{1,0:T(8,128)} collective-permute-done((f32[4096,1024]{1,0:T(8,128)S(1)}, f32[4096,1024]{1,0:T(8,128)}, u32[]{:S(2)}, u32[]{:S(2)}) %collective-permute-start.2) | collective-permute-done | bytes 16777248 | tf_op jit(solution)/shard_map/ppermute | solution.py:26
  813.6 12.4 add.27
  826.0 2.5 collective-permute-start.3
  828.6 719.1 %collective-permute-done.3 = f32[4096,1024]{1,0:T(8,128)} collective-permute-done((f32[4096,1024]{1,0:T(8,128)}, f32[4096,1024]{1,0:T(8,128)}, u32[]{:S(2)}, u32[]{:S(2)}) %collective-permute-start.3) | collective-permute-done | bytes 16777248 | tf_op jit(solution)/shard_map/ppermute | solution.py:26
  1547.6 4.2 fusion
  1551.8 0.0 copy-start.1
  1551.8 0.0 all-reduce.2.cloned.1.call-update
  1551.8 0.2 reduce-scatter.2.cloned.1.call-start
  1552.1 63.6 %all-reduce.2.cloned.1.call-done = f32[512,1024]{1,0:T(8,128)} async-done(((f32[512,1024]{1,0:T(8,128)}), f32[512,1024]{1,0:T(8,128)}) %all-reduce.2.cloned.1.call-update) | async-done | bytes 2097168 | tf_op jit(solution)/shard_map/psum | solution.py:9
  1615.6 0.0 copy-done.1
  1615.6 0.0 copy-start.2
  1615.6 2.2 multiply_subtract_fusion
  1617.8 0.1 copy-done.2
  1617.9 1.9 fusion.3
  1619.8 0.0 copy-start
  1619.8 1.9 fusion.5
  1621.7 0.0 copy-done
  1621.7 1.9 fusion.2
  1623.6 1.9 fusion.1
  1625.4 1.5 pad_maximum_fusion.1
  1627.0 0.0 reduce-scatter.2.cloned.1.call-update
  1627.0 1.5 pad_maximum_fusion
  1628.5 2.9 copy.6
  1631.3 57.3 %reduce-scatter.2.cloned.1.call-done = f32[2,32,512]{2,1,0:T(8,128)} async-done(((f32[2,512,512]{2,1,0:T(8,128)}), f32[2,32,512]{2,1,0:T(8,128)}) %reduce-scatter.2.cloned.1.call-update) | async-done | bytes 131088 | tf_op jit(solution)/shard_map/reduce_scatter | solution.py:53
Async XLA Ops:
  7.2 1608.5 %all-reduce.2.cloned.1.call-start = ((), (), s32[]{:S(2)}) async-start(), calls=%async_computation.1 | async-start | bytes 4194304 | tf_op jit(solution)/shard_map/psum | solution.py:9
  38.4 25.4 %collective-permute-start = (f32[4096,1024]{1,0:T(8,128)S(1)}, f32[4096,1024]{1,0:T(8,128)}, u32[]{:S(2)}, u32[]{:S(2)}) collective-permute-start(f32[4096,1024]{1,0:T(8,128)S(1)} %fusion.13), channel_id=1, source_target_pairs={{0,2},{2,0},{4,6},{6,4},{8,10},{10,8},{12,14},{14,12},{16,18},{18,... | collective-permute-start | bytes 50331656 | tf_op jit(solution)/shard_map/ppermute | solution.py:26
  76.2 363.7 %collective-permute-start.1 = (f32[4096,1024]{1,0:T(8,128)}, f32[4096,1024]{1,0:T(8,128)}, u32[]{:S(2)}, u32[]{:S(2)}) collective-permute-start(f32[4096,1024]{1,0:T(8,128)} %add.25), channel_id=1, source_target_pairs={{0,4},{2,6},{4,0},{6,2},{8,12},{10,14},{12,8},{14,10},{16,20},{18,... | collective-permute-start | bytes 50331656 | tf_op jit(solution)/shard_map/ppermute | solution.py:26
  451.7 361.9 %collective-permute-start.2 = (f32[4096,1024]{1,0:T(8,128)S(1)}, f32[4096,1024]{1,0:T(8,128)}, u32[]{:S(2)}, u32[]{:S(2)}) collective-permute-start(f32[4096,1024]{1,0:T(8,128)S(1)} %add.26), channel_id=1, source_target_pairs={{0,8},{2,10},{4,12},{6,14},{8,0},{10,2},{12,4},{14,6},{16,24},{18,... | collective-permute-start | bytes 50331656 | tf_op jit(solution)/shard_map/ppermute | solution.py:26
  826.0 721.6 %collective-permute-start.3 = (f32[4096,1024]{1,0:T(8,128)}, f32[4096,1024]{1,0:T(8,128)}, u32[]{:S(2)}, u32[]{:S(2)}) collective-permute-start(f32[4096,1024]{1,0:T(8,128)} %add.27), channel_id=1, source_target_pairs={{0,16},{2,18},{4,20},{6,22},{8,24},{10,26},{12,28},{14,30},{16,0},... | collective-permute-start | bytes 50331656 | tf_op jit(solution)/shard_map/ppermute | solution.py:26
  1551.8 63.8 %copy-start.1 = (f32[512,1024]{1,0:T(8,128)S(1)}, f32[512,1024]{1,0:T(8,128)}, u32[]{:S(2)}) copy-start(f32[512,1024]{1,0:T(8,128)} %param.6) | copy-start | bytes 6291460
  1551.8 136.8 %reduce-scatter.2.cloned.1.call-start = ((), (), s32[]{:S(2)}) async-start(), calls=%async_computation.2 | async-start | bytes 2228224 | tf_op jit(solution)/shard_map/reduce_scatter | solution.py:53
  1615.6 2.2 copy-start.2
  1619.8 1.9 copy-start
Sparse Core Ops, SparseCore 0:
  1552.0 63.6 all-reduce.1
  1627.1 61.5 reduce-scatter.1
